TPU v7x, 256 devices: a whole 4x4x8 slice. The times are simulated.
256 devices in a mesh: tok: 16 (over x, y_hi, core), col: 8 (over z), grp: 2 (over y_lo).
Axes of the slice: x: 4, y: 4 (y_hi: 2, y_lo: 2; y = y_hi * 2 + y_lo), z: 8, core: 2. Of those that a mesh axis runs over, the one named last changes fastest.
Arguments:
- calibration: bfloat16 [24576, 4096], P(('tok', 'grp'), 'col'), may hold values from -1.1 to 1.1
- weight: float32 [4096, 4096], P(('tok', 'grp'), 'col'), may hold values from -6 to 6
- tile_mask: int32 [32, 32], P(('tok', 'grp'), 'col'), may hold values 0 or 1
- token_ids: int32 [2048], P(('tok', 'grp')), may hold values from 0 to 767
Outputs:
- new_weight: bfloat16 [4096, 4096], P(('tok', 'grp'), 'col')
- outputs: bfloat16 [2048, 4096], P('col', ('tok', 'grp'))
All inputs are finite; a program needn't handle non-finite values. No bound on the sum of `tile_mask` on one device may be relied on, other than what follows from the above.
Results may differ from a plain program's by a relative error of at most 0.0019.
The roundings to bfloat16 on the way count: a program that leaves them out, or rounds other values in their place, can miss the bound.
Values may be sent and summed in bfloat16 or wider, within the bound.
No kernel may reach another device: no remote copies, remote signals or barrier semaphores. Data moves between devices by JAX's collectives and lax.ppermute only.
A program may use at most 64 MiB of HBM per device.

v0:
```python
import jax
import jax.numpy as jnp
from jax import lax
from jax.sharding import PartitionSpec as P

TILE = 128
ITERS = 3
DAMPING = 0.1


def expand_tiles(tile_flags):
    tile_rows, tile_cols = tile_flags.shape
    expanded = jnp.broadcast_to(
        tile_flags.astype(jnp.float32)[:, None, :, None], (tile_rows, TILE, tile_cols, TILE)
    )
    return expanded.reshape(tile_rows * TILE, tile_cols * TILE)


def per_device(calibration, weight, tile_mask, token_ids):
    col_width = calibration.shape[1]
    col_count = lax.axis_size("col")
    width = col_width * col_count
    col_place = lax.axis_index("col")
    squares = jnp.sum(jnp.square(calibration.astype(jnp.float32)))
    trace_total = lax.psum(squares, ("tok", "col", "grp"))
    partial_gram = lax.dot_general(
        calibration,
        lax.all_gather(calibration, "col", axis=1, tiled=True),
        (((0,), (0,)), ((), ())),
        preferred_element_type=jnp.float32,
    )
    gram_slice = lax.psum_scatter(partial_gram, ("tok", "grp"), scatter_dimension=1, tiled=True)
    gram_rows = lax.all_gather(gram_slice, ("tok", "grp"), axis=1, tiled=True)
    trace_scale = trace_total / width
    row_ids = col_place * col_width + lax.broadcasted_iota(jnp.int32, gram_rows.shape, 0)
    col_ids = lax.broadcasted_iota(jnp.int32, gram_rows.shape, 1)
    stationary = gram_rows / trace_scale + jnp.where(row_ids == col_ids, DAMPING, 0.0)

    def apply_gram(operand):
        return lax.dot_general(
            lax.all_gather(operand, "col", axis=1, tiled=True),
            stationary,
            (((1,), (1,)), ((), ())),
            precision=lax.Precision.HIGHEST,
            preferred_element_type=jnp.float32,
        )

    keep_mask = expand_tiles(tile_mask)
    current = weight * keep_mask
    residual = apply_gram(current - weight)
    for iteration in range(ITERS):
        gradient = residual * keep_mask
        image_rows = apply_gram(gradient)
        sums_pair = lax.psum(
            (jnp.sum(gradient * gradient), jnp.sum(gradient * image_rows)), ("tok", "col", "grp")
        )
        length = sums_pair[0] / sums_pair[1]
        current = current - length * gradient
        if iteration + 1 < ITERS:
            residual = residual - length * image_rows
    new_weight = current.astype(jnp.bfloat16)
    chosen = jnp.take(calibration, token_ids, axis=0)
    all_chosen = lax.all_gather(chosen, ("tok", "grp"), axis=0, tiled=True)
    outputs = lax.psum_scatter(
        lax.dot_general(
            all_chosen, new_weight, (((1,), (1,)), ((), ())), preferred_element_type=jnp.float32
        ),
        "col",
        scatter_dimension=0,
        tiled=True,
    )
    return (new_weight, outputs.astype(jnp.bfloat16))


def solution(mesh):
    placed = (
        P(("tok", "grp"), "col"),
        P(("tok", "grp"), "col"),
        P(("tok", "grp"), "col"),
        P(("tok", "grp")),
    )
    return jax.shard_map(
        per_device,
        mesh=mesh,
        in_specs=placed,
        out_specs=(P(("tok", "grp"), "col"), P("col", ("tok", "grp"))),
        check_vma=False,
    )
```

profile of v0, /device:TPU:2, one launch (start us, length us, event | category | flops | bytes accessed | tf_op | source)
XLA Modules:
  0.0 833.4 jit_solution(12873526358352657317)
XLA Ops:
  7.9 79.3 %all-gather.10.cloned.1.call-done = bf16[768,4096]{1,0:T(8,128)(2,1)} async-done(((bf16[768,512]{1,0:T(8,128)(2,1)}), bf16[768,4096]{1,0:T(8,128)(2,1)}) %all-gather.10.cloned.1.call-update) | async-done | bytes 6291472 | tf_op jit(solution)/shard_map/all_gather | solution.py:28
  87.3 9.7 %fusion.4 = f32[512,4096]{1,0:T(8,128)} fusion(bf16[768,512]{1,0:T(8,128)(2,1)} %param.4, bf16[768,4096]{1,0:T(8,128)(2,1)} %all-gather.10.cloned.1.call-done), kind=kOutput, calls=%fused_computation.27 | convolution fusion | flops 3221225472 | bytes 15466496 | tf_op jit(solution)/shard_map/dot_general | solution.py:26
  97.1 143.3 %reduce-scatter.3.cloned.1.call-done = f32[512,128]{1,0:T(8,128)} async-done(((f32[512,4096]{1,0:T(8,128)}), f32[512,128]{1,0:T(8,128)}) %reduce-scatter.3.cloned.1.call-update) | async-done | bytes 262160 | tf_op jit(solution)/shard_map/reduce_scatter | solution.py:32
  240.6 0.7 multiply_subtract_fusion.1
  241.4 1.0 multiply_reduce_fusion
  242.4 77.8 %psum.49 = f32[]{:T(128)} all-reduce(f32[]{:T(128)} %multiply_reduce_fusion), channel_id=1, replica_groups=mesh['tok'=16,'col'=8,'grp'=2] {'tok','col','grp'}, use_global_device_ids=true, to_apply=%region_2.0 | all-reduce | flops 1 | bytes 8 | tf_op jit(solution)/shard_map/psum | solution.py:25
  320.8 22.7 %all-gather.12.cloned.1.call-done = f32[512,4096]{1,0:T(8,128)} async-done(((f32[512,128]{1,0:T(8,128)}), f32[512,4096]{1,0:T(8,128)}) %all-gather.12.cloned.1.call-update) | async-done | bytes 8388624 | tf_op jit(solution)/shard_map/all_gather | solution.py:33
  343.5 6.3 select_add_fusion
  349.8 36.7 %all-gather.8.cloned.1.call-done = f32[128,4096]{1,0:T(8,128)} async-done(((f32[128,512]{1,0:T(8,128)}), f32[128,4096]{1,0:T(8,128)}) %all-gather.8.cloned.1.call-update) | async-done | bytes 2097168 | tf_op jit(solution)/shard_map/all_gather | solution.py:41
  386.5 13.5 %broadcast_multiply_fusion.1 = (f32[128,512]{1,0:T(8,128)}, f32[128,512]{1,0:T(8,128)S(1)}) fusion(f32[512]{0:T(512)S(1)} %broadcast_bitcast_fusion, f32[128,4096]{1,0:T(8,128)} %all-gather.8.cloned.1.call-done, f32[512,4096]{1,0:T(8,128)} %select_add_fusion), kind=kOutput, calls=%fused_computation.19 | convolution fusion | flops 3221291008 | bytes 11012096 | tf_op jit(solution)/shard_map/dot_general | solution.py:40
  400.6 39.3 %all-gather.14.cloned.1.call-done = f32[128,4096]{1,0:T(8,128)} async-done(((f32[128,512]{1,0:T(8,128)}), f32[128,4096]{1,0:T(8,128)}) %all-gather.14.cloned.1.call-update) | async-done | bytes 2097168 | tf_op jit(solution)/shard_map/all_gather | solution.py:41
  439.8 13.4 %multiply_reduce_fusion.4 = (f32[]{:T(128)}, f32[]{:T(128)}, f32[128,512]{1,0:T(8,128)S(1)}) fusion(f32[128,512]{1,0:T(8,128)} %get-tuple-element.14, f32[128,4096]{1,0:T(8,128)} %all-gather.14.cloned.1.call-done, f32[512,4096]{1,0:T(8,128)} %select_add_fusion), kind=kOutput, calls=%fused_computation.16 | convolution fusion | flops 3221487616 | bytes 11010056 | tf_op jit(solution)/shard_map/dot_general | solution.py:40
  453.2 74.2 %all-reduce.2 = (f32[]{:T(128)}, f32[]{:T(128)}) all-reduce(f32[]{:T(128)} %get-tuple-element.5, f32[]{:T(128)} %get-tuple-element.4), channel_id=1, replica_groups=mesh['tok'=16,'col'=8,'grp'=2] {'tok','col','grp'}, use_global_device_ids=true, to_apply=%region_4.5 | all-reduce | flops 2 | bytes 16 | tf_op jit(solution)/shard_map/psum | solution.py:54
  528.7 0.8 broadcast_multiply_fusion
  529.8 37.6 %all-gather.16.cloned.1.call-done = f32[128,4096]{1,0:T(8,128)} async-done(((f32[128,512]{1,0:T(8,128)}), f32[128,4096]{1,0:T(8,128)}) %all-gather.16.cloned.1.call-update) | async-done | bytes 2097168 | tf_op jit(solution)/shard_map/all_gather | solution.py:41
  567.4 13.4 %multiply_reduce_fusion.2 = (f32[]{:T(128)}, f32[]{:T(128)}, f32[128,512]{1,0:T(8,128)S(1)}) fusion(f32[128,512]{1,0:T(8,128)} %broadcast_multiply_fusion, f32[128,4096]{1,0:T(8,128)} %all-gather.16.cloned.1.call-done, f32[512,4096]{1,0:T(8,128)} %select_add_fusion), kind=kOutput, calls=%fused_computation.13 | convolution fusion | flops 3221487616 | bytes 11010056 | tf_op jit(solution)/shard_map/dot_general | solution.py:40
  580.8 74.2 %all-reduce.1 = (f32[]{:T(128)}, f32[]{:T(128)}) all-reduce(f32[]{:T(128)} %get-tuple-element.3, f32[]{:T(128)} %get-tuple-element.2), channel_id=1, replica_groups=mesh['tok'=16,'col'=8,'grp'=2] {'tok','col','grp'}, use_global_device_ids=true, to_apply=%region_8.9 | all-reduce | flops 2 | bytes 16 | tf_op jit(solution)/shard_map/psum | solution.py:54
  656.3 1.4 multiply_reduce_fusion.1
  659.6 36.1 %all-gather.18.cloned.1.call-done = f32[128,4096]{1,0:T(8,128)} async-done(((f32[128,512]{1,0:T(8,128)}), f32[128,4096]{1,0:T(8,128)}) %all-gather.18.cloned.1.call-update) | async-done | bytes 2097168 | tf_op jit(solution)/shard_map/all_gather | solution.py:41
  695.7 13.4 %fusion = f32[]{:T(128)} fusion(f32[128,512]{1,0:T(8,128)} %get-tuple-element.13, f32[128,4096]{1,0:T(8,128)} %all-gather.18.cloned.1.call-done, f32[512,4096]{1,0:T(8,128)} %select_add_fusion), kind=kOutput, calls=%fused_computation.5 | convolution fusion | flops 3221356544 | bytes 10747908 | tf_op jit(solution)/shard_map/dot_general | solution.py:40
  709.0 74.2 %all-reduce = (f32[]{:T(128)}, f32[]{:T(128)}) all-reduce(f32[]{:T(128)} %get-tuple-element.12, f32[]{:T(128)} %fusion), channel_id=1, replica_groups=mesh['tok'=16,'col'=8,'grp'=2] {'tok','col','grp'}, use_global_device_ids=true, to_apply=%region_12.13 | all-reduce | flops 2 | bytes 16 | tf_op jit(solution)/shard_map/psum | solution.py:54
  784.8 3.3 fusion.5
  788.1 37.0 %reduce-scatter.5.cloned.1.call-done = f32[256,128]{1,0:T(8,128)} async-done(((f32[2048,128]{1,0:T(8,128)}), f32[256,128]{1,0:T(8,128)}) %reduce-scatter.5.cloned.1.call-update) | async-done | bytes 131088 | tf_op jit(solution)/shard_map/reduce_scatter | solution.py:64
  825.1 1.5 convert_element_type.15
  (44 shorter events, 3.8 us)
Async XLA Ops:
  7.2 80.1 %all-gather.10.cloned.1.call-start = ((), (), s32[]{:S(2)}) async-start(), calls=%async_computation.3 | async-start | bytes 7077888 | tf_op jit(solution)/shard_map/all_gather | solution.py:28
  7.9 232.5 %reduce-scatter.3.cloned.1.call-start = ((), (), s32[]{:S(2)}) async-start(), calls=%async_computation.4 | async-start | bytes 8650752 | tf_op jit(solution)/shard_map/reduce_scatter | solution.py:32
  97.0 143.5 %copy-start.6 = (s32[1,4]{1,0:T(1,128)S(1)}, s32[1,4]{1,0:T(1,128)}, u32[]{:S(2)}) copy-start(s32[1,4]{1,0:T(1,128)} %param.6) | copy-start | bytes 52
  97.0 143.6 %copy-start.4 = (f32[128,512]{1,0:T(8,128)S(1)}, f32[128,512]{1,0:T(8,128)}, u32[]{:S(2)}) copy-start(f32[128,512]{1,0:T(8,128)} %param.5) | copy-start | bytes 786436
  97.0 144.4 %copy-start = (bf16[768,512]{1,0:T(8,128)(2,1)S(1)}, bf16[768,512]{1,0:T(8,128)(2,1)}, u32[]{:S(2)}) copy-start(bf16[768,512]{1,0:T(8,128)(2,1)} %param.4) | copy-start | bytes 2359300
  97.0 246.5 %all-gather.12.cloned.1.call-start = ((), (), s32[]{:S(2)}) async-start(), calls=%async_computation.5 | async-start | bytes 8650752 | tf_op jit(solution)/shard_map/all_gather | solution.py:33
  240.4 146.1 %all-gather.8.cloned.1.call-start = ((), (), s32[]{:S(2)}) async-start(), calls=%async_computation.2 | async-start | bytes 2359296 | tf_op jit(solution)/shard_map/all_gather | solution.py:41
  241.3 198.5 %all-gather.14.cloned.1.call-start = ((), (), s32[]{:S(2)}) async-start(), calls=%async_computation.6 | async-start | bytes 2359296 | tf_op jit(solution)/shard_map/all_gather | solution.py:41
  400.0 167.4 %all-gather.16.cloned.1.call-start = ((), (), s32[]{:S(2)}) async-start(), calls=%async_computation.7 | async-start | bytes 2359296 | tf_op jit(solution)/shard_map/all_gather | solution.py:41
  529.5 128.3 %copy-start.7 = (s32[64]{0:T(128)S(1)}, s32[64]{0:T(128)}, u32[]{:S(2)}) copy-start(s32[64]{0:T(128)} %param.7) | copy-start | bytes 772
  529.5 166.1 %all-gather.18.cloned.1.call-start = ((), (), s32[]{:S(2)}) async-start(), calls=%async_computation.8 | async-start | bytes 2359296 | tf_op jit(solution)/shard_map/all_gather | solution.py:41
  656.3 128.3 %copy-start.1 = (f32[128,512]{1,0:T(8,128)S(1)}, f32[128,512]{1,0:T(8,128)}, u32[]{:S(2)}) copy-start(f32[128,512]{1,0:T(8,128)} %get-tuple-element.14) | copy-start | bytes 786436
  656.3 128.3 %copy-start.3 = (f32[128,512]{1,0:T(8,128)S(1)}, f32[128,512]{1,0:T(8,128)}, u32[]{:S(2)}) copy-start(f32[128,512]{1,0:T(8,128)} %broadcast_multiply_fusion) | copy-start | bytes 786436
  657.7 126.9 %copy-start.2 = (f32[128,512]{1,0:T(8,128)S(1)}, f32[128,512]{1,0:T(8,128)}, u32[]{:S(2)}) copy-start(f32[128,512]{1,0:T(8,128)} %get-tuple-element.13) | copy-start | bytes 786436
  657.8 127.0 %all-gather.20.cloned.1.call-start = ((), (), s32[]{:S(2)}) async-start(), calls=%async_computation.9 | async-start | bytes 2162688 | tf_op jit(solution)/shard_map/all_gather | solution.py:63
  659.3 165.8 %reduce-scatter.5.cloned.1.call-start = ((), (), s32[]{:S(2)}) async-start(), calls=%async_computation.10 | async-start | bytes 1179648 | tf_op jit(solution)/shard_map/reduce_scatter | solution.py:64
  784.8 41.9 %copy-start.5 = (bf16[128,512]{1,0:T(8,128)(2,1)}, bf16[128,512]{1,0:T(8,128)(2,1)S(1)}, u32[]{:S(2)}) copy-start(bf16[128,512]{1,0:T(8,128)(2,1)S(1)} %fusion.3) | copy-start | bytes 393220
Sparse Core Ops, SparseCore 0:
  9.8 77.4 all-gather.9
  97.2 143.1 reduce-scatter.2
  242.1 101.3 all-gather.11
  345.2 41.3 all-gather.7
  400.1 39.6 all-gather.13
  529.7 37.7 all-gather.15
  657.9 37.7 all-gather.17
  698.0 84.5 all-gather.19
  788.3 36.8 reduce-scatter.4
where the time goes:
time: 838 us; the launch traced here: 833 us
  waiting for transfers between devices  433 us (52%)
  blocking collectives  300 us (36%)
  matrix products  66.6 us (8%)
  between operations  18.9 us (2%)
  other arithmetic  12.6 us (2%)
    psum x3, blocking collectives, per_device(): lax.psum((jnp.sum(gradient * gradient), jnp.sum(gradient * image_rows)),...  223 us
    all_gather x4, waiting for transfers between devices, apply_gram(): lax.all_gather(operand, 'col', axis=1, tiled=True)  150 us
    reduce_scatter x1, waiting for transfers between devices, per_device(): lax.psum_scatter(partial_gram, ('tok', 'grp'), scatter_dimension=1, tiled...  143 us
    all_gather x1, waiting for transfers between devices, per_device(): lax.all_gather(calibration, 'col', axis=1, tiled=True)  79.3 us
    psum x1, blocking collectives, per_device(): trace_total = lax.psum(squares, ('tok', 'col', 'grp'))  77.8 us
    dot_general x4, matrix products, apply_gram(): lax.dot_general(lax.all_gather(operand, 'col', axis=1, tiled=True), stati...  53.5 us
    reduce_scatter x1, waiting for transfers between devices, per_device(): lax.psum_scatter(lax.dot_general(all_chosen, new_weight, (((1,), (1,)), (...  37 us
    all_gather x1, waiting for transfers between devices, per_device(): gram_rows = lax.all_gather(gram_slice, ('tok', 'grp'), axis=1, tiled=True)  22.7 us
  transfers between devices with their start and end apart: 9, of which 8 were waited for; matrix products, arithmetic and copies ran while one was open for 3% of the time, Pallas kernels for 0%

commit v1 on v0

--- a/solution.py
+++ b/solution.py
@@ -6,6 +6,19 @@
 TILE = 128
 ITERS = 3
 DAMPING = 0.1
+
+
+def collect(value, axis, dim):
+    ways = lax.axis_size(axis)
+    up = [(d, (d + 1) % ways) for d in range(ways)]
+    down = [(d, (d - 1) % ways) for d in range(ways)]
+    earlier, later = ([value], [value])
+    for _ in range(ways // 2):
+        earlier.append(lax.ppermute(earlier[-1], axis, up))
+    for _ in range((ways - 1) // 2):
+        later.append(lax.ppermute(later[-1], axis, down))
+    line = jnp.concatenate([*earlier[::-1], *later[1:]], axis=dim)
+    return jnp.roll(line, (lax.axis_index(axis) - ways // 2) * value.shape[dim], axis=dim)
 
 
 def expand_tiles(tile_flags):
@@ -38,7 +51,7 @@
 
     def apply_gram(operand):
         return lax.dot_general(
-            lax.all_gather(operand, "col", axis=1, tiled=True),
+            collect(operand, "col", 1),
             stationary,
             (((1,), (1,)), ((), ())),
             precision=lax.Precision.HIGHEST,

time: 838 us -> 787 us (0.939)
  waiting for transfers between devices: 433 us -> 344 us
  starting transfers between devices: 1.27 us -> 38.9 us
    all_gather x4 -> x0, waiting for transfers between devices: 150 us -> none  [apply_gram(): lax.all_gather(operand, 'col', axis=1, tiled=True)]
    ppermute x0 -> x28, waiting for transfers between devices: none -> 85.4 us  [the longest x16 82.6 us: collect(): earlier.append(lax.ppermute(earlier[-1], axis, up))]
    ppermute x0 -> x28, starting transfers between devices: none -> 38.7 us  [the longest x12 36.9 us: collect(): later.append(lax.ppermute(later[-1], axis, down))]
    all_gather x1, waiting for transfers between devices: 22.7 us -> 0.01 us  [per_device(): gram_rows = lax.all_gather(gram_slice, ('tok', 'grp'), axis=1, tiled=True)]
  transfers between devices with their start and end apart: 9 -> 33, of which waited for: 8 -> 19; matrix products, arithmetic and copies ran while one was open for 3% -> 5% of each run, Pallas kernels for 0% -> 0%
where the time goes in v1:
time: 787 us; the launch traced here: 779 us
  waiting for transfers between devices  344 us (44%)
  blocking collectives  304 us (39%)
  matrix products  60 us (8%)
  starting transfers between devices  38.9 us (5%)
  between operations  19 us (2%)
    psum x3, blocking collectives, per_device(): lax.psum((jnp.sum(gradient * gradient), jnp.sum(gradient * image_rows)),...  224 us
    reduce_scatter x1, waiting for transfers between devices, per_device(): lax.psum_scatter(partial_gram, ('tok', 'grp'), scatter_dimension=1, tiled...  143 us
    ppermute x16, waiting for transfers between devices, collect(): earlier.append(lax.ppermute(earlier[-1], axis, up))  82.6 us
    psum x1, blocking collectives, per_device(): trace_total = lax.psum(squares, ('tok', 'col', 'grp'))  80.1 us
    all_gather x1, waiting for transfers between devices, per_device(): lax.all_gather(calibration, 'col', axis=1, tiled=True)  79.3 us
    dot_general x4, matrix products, apply_gram(): lax.dot_general(collect(operand, 'col', 1), stationary, (((1,), (1,)), ((...  47 us
    ppermute x12, starting transfers between devices, collect(): later.append(lax.ppermute(later[-1], axis, down))  36.9 us
    reduce_scatter x1, waiting for transfers between devices, per_device(): lax.psum_scatter(lax.dot_general(all_chosen, new_weight, (((1,), (1,)), (...  35.3 us
  transfers between devices with their start and end apart: 33, of which 19 were waited for; matrix products, arithmetic and copies ran while one was open for 5% of the time, Pallas kernels for 0%

profile of v1, /device:TPU:2, one launch (start us, length us, event | category | flops | bytes accessed | tf_op | source)
XLA Modules:
  0.0 778.7 jit_solution(2967947603523120423)
XLA Ops:
  7.9 79.3 %all-gather.4.cloned.1.call-done = bf16[768,4096]{1,0:T(8,128)(2,1)} async-done(((bf16[768,512]{1,0:T(8,128)(2,1)}), bf16[768,4096]{1,0:T(8,128)(2,1)}) %all-gather.4.cloned.1.call-update) | async-done | bytes 6291472 | tf_op jit(solution)/shard_map/all_gather | solution.py:41
  87.3 9.8 %fusion.29 = f32[512,4096]{1,0:T(8,128)} fusion(bf16[768,512]{1,0:T(8,128)(2,1)} %param.6, bf16[768,4096]{1,0:T(8,128)(2,1)} %all-gather.4.cloned.1.call-done), kind=kOutput, calls=%fused_computation.83 | convolution fusion | flops 3221225472 | bytes 15466496 | tf_op jit(solution)/shard_map/dot_general | solution.py:39
  97.1 143.3 %reduce-scatter.3.cloned.1.call-done = f32[512,128]{1,0:T(8,128)} async-done(((f32[512,4096]{1,0:T(8,128)}), f32[512,128]{1,0:T(8,128)}) %reduce-scatter.3.cloned.1.call-update) | async-done | bytes 262160 | tf_op jit(solution)/shard_map/reduce_scatter | solution.py:45
  242.2 7.7 collective-permute-done
  253.2 5.0 collective-permute-done.1
  261.5 4.3 collective-permute-done.2
  266.8 80.1 %psum.49 = f32[]{:T(128)} all-reduce(f32[]{:T(128)} %multiply_reduce_fusion), channel_id=1, replica_groups=mesh['tok'=16,'col'=8,'grp'=2] {'tok','col','grp'}, use_global_device_ids=true, to_apply=%region_2.4 | all-reduce | flops 1 | bytes 8 | tf_op jit(solution)/shard_map/psum | solution.py:38
  356.6 12.3 %broadcast_multiply_fusion.1 = (f32[128,512]{1,0:T(8,128)S(1)}, f32[128,512]{1,0:T(8,128)S(1)}) fusion(f32[512]{0:T(512)S(1)} %broadcast_bitcast_fusion, f32[512,4096]{1,0:T(8,128)} %all-gather.6.cloned.1.call-done, s32[512]{0:T(512)S(1)} %iota_add_fusion, f32[]{:T(128)S(6)} %div.18, s32[]{:T(128)S(6)} %select_n.33, ...), kind=kOutput, calls=%fused_computation.35 | convolution fusion | flops 3230203904 | bytes 11014152 | tf_op jit(solution)/shard_map/dot_general | solution.py:53
  369.1 8.4 %collective-permute-done.7 = f32[128,512]{1,0:T(8,128)S(1)} collective-permute-done((f32[128,512]{1,0:T(8,128)S(1)}, f32[128,512]{1,0:T(8,128)S(1)}, u32[]{:S(2)}, u32[]{:S(2)}) %collective-permute-start.7) | collective-permute-done | bytes 262176 | tf_op jit(solution)/shard_map/ppermute | solution.py:17
  380.7 4.3 collective-permute-done.8
  388.3 4.7 collective-permute-done.9
  400.8 9.6 %multiply_reduce_fusion.4 = (f32[]{:T(128)}, f32[]{:T(128)}, f32[128,512]{1,0:T(8,128)S(1)}) fusion(f32[128,512]{1,0:T(8,128)S(1)} %get-tuple-element.15, f32[512,4096]{1,0:T(8,128)S(1)} %copy-done.3, s32[512]{0:T(512)S(1)} %iota_add_fusion, f32[]{:T(128)S(6)} %div.18, s32[]{:T(128)S(6)} %select_n.33, f32[128,4096]{1,0:T(8,128)S(1)} %constant_dynamic-update-slice_fusion.8), kind=kOutput, calls=%fused_computation.32 | convolution fusion | flops 3230400512 | bytes 11012112 | tf_op jit(solution)/shard_map/dot_general | solution.py:53
  410.4 75.2 %all-reduce.2 = (f32[]{:T(128)}, f32[]{:T(128)}) all-reduce(f32[]{:T(128)} %get-tuple-element.6, f32[]{:T(128)} %get-tuple-element.5), channel_id=1, replica_groups=mesh['tok'=16,'col'=8,'grp'=2] {'tok','col','grp'}, use_global_device_ids=true, to_apply=%region_4.6 | all-reduce | flops 2 | bytes 16 | tf_op jit(solution)/shard_map/psum | solution.py:67
  487.1 9.2 %collective-permute-done.14 = f32[128,512]{1,0:T(8,128)S(1)} collective-permute-done((f32[128,512]{1,0:T(8,128)S(1)}, f32[128,512]{1,0:T(8,128)S(1)}, u32[]{:S(2)}, u32[]{:S(2)}) %collective-permute-start.14) | collective-permute-done | bytes 262176 | tf_op jit(solution)/shard_map/ppermute | solution.py:17
  499.5 5.1 collective-permute-done.15
  521.1 12.2 %multiply_reduce_fusion.2 = (f32[]{:T(128)}, f32[]{:T(128)}, f32[128,512]{1,0:T(8,128)S(1)}) fusion(f32[128,512]{1,0:T(8,128)S(1)} %broadcast_multiply_fusion, f32[512,4096]{1,0:T(8,128)} %all-gather.6.cloned.1.call-done, s32[512]{0:T(512)S(1)} %iota_add_fusion, f32[]{:T(128)S(6)} %div.18, s32[]{:T(128)S(6)} %select_n.33, ...), kind=kOutput, calls=%fused_computation.29 | convolution fusion | flops 3230400512 | bytes 11012112 | tf_op jit(solution)/shard_map/dot_general | solution.py:53
  533.3 74.1 %all-reduce.1 = (f32[]{:T(128)}, f32[]{:T(128)}) all-reduce(f32[]{:T(128)} %get-tuple-element.4, f32[]{:T(128)} %get-tuple-element.3), channel_id=1, replica_groups=mesh['tok'=16,'col'=8,'grp'=2] {'tok','col','grp'}, use_global_device_ids=true, to_apply=%region_8.10 | all-reduce | flops 2 | bytes 16 | tf_op jit(solution)/shard_map/psum | solution.py:67
  609.4 9.2 %collective-permute-done.21 = f32[128,512]{1,0:T(8,128)S(1)} collective-permute-done((f32[128,512]{1,0:T(8,128)S(1)}, f32[128,512]{1,0:T(8,128)S(1)}, u32[]{:S(2)}, u32[]{:S(2)}) %collective-permute-start.21) | collective-permute-done | bytes 262176 | tf_op jit(solution)/shard_map/ppermute | solution.py:17
  621.9 5.1 collective-permute-done.22
  630.3 4.3 collective-permute-done.23
  638.0 4.2 collective-permute-done.24
  642.4 13.0 %fusion.15 = f32[]{:T(128)} fusion(f32[128,512]{1,0:T(8,128)S(1)} %get-tuple-element.14, s32[]{:T(128)S(6)} %select_n.33, f32[128,4096]{1,0:T(8,128)S(1)} %constant_dynamic-update-slice_fusion.24, f32[512,4096]{1,0:T(8,128)} %all-gather.6.cloned.1.call-done, s32[512]{0:T(512)S(1)} %iota_add_fusion, f32[]{:T(128)S(6)} %div.18), kind=kOutput, calls=%fused_computation.21 | convolution fusion | flops 3230269440 | bytes 10749964 | tf_op jit(solution)/shard_map/dot_general | solution.py:53
  655.4 74.9 %all-reduce = (f32[]{:T(128)}, f32[]{:T(128)}) all-reduce(f32[]{:T(128)} %get-tuple-element.13, f32[]{:T(128)} %fusion.15), channel_id=1, replica_groups=mesh['tok'=16,'col'=8,'grp'=2] {'tok','col','grp'}, use_global_device_ids=true, to_apply=%region_12.14 | all-reduce | flops 2 | bytes 16 | tf_op jit(solution)/shard_map/psum | solution.py:67
  735.1 35.3 %reduce-scatter.5.cloned.1.call-done = f32[256,128]{1,0:T(8,128)} async-done(((f32[2048,128]{1,0:T(8,128)}), f32[256,128]{1,0:T(8,128)}) %reduce-scatter.5.cloned.1.call-update) | async-done | bytes 131088 | tf_op jit(solution)/shard_map/reduce_scatter | solution.py:77
  (115 shorter events, 68.9 us)
Async XLA Ops:
  7.2 80.1 %all-gather.4.cloned.1.call-start = ((), (), s32[]{:S(2)}) async-start(), calls=%async_computation.2 | async-start | bytes 7077888 | tf_op jit(solution)/shard_map/all_gather | solution.py:41
  7.9 232.5 %reduce-scatter.3.cloned.1.call-start = ((), (), s32[]{:S(2)}) async-start(), calls=%async_computation.3 | async-start | bytes 8650752 | tf_op jit(solution)/shard_map/reduce_scatter | solution.py:45
  97.0 259.6 %all-gather.6.cloned.1.call-start = ((), (), s32[]{:S(2)}) async-start(), calls=%async_computation.4 | async-start | bytes 8650752 | tf_op jit(solution)/shard_map/all_gather | solution.py:46
  240.4 491.4 %all-gather.8.cloned.1.call-start = ((), (), s32[]{:S(2)}) async-start(), calls=%async_computation.5 | async-start | bytes 2162688 | tf_op jit(solution)/shard_map/all_gather | solution.py:76
  240.6 9.3 %collective-permute-start = (f32[128,512]{1,0:T(8,128)S(1)}, f32[128,512]{1,0:T(8,128)S(1)}, u32[]{:S(2)}, u32[]{:S(2)}) collective-permute-start(f32[128,512]{1,0:T(8,128)S(1)} %multiply_subtract_fusion.1), channel_id=1, source_target_pairs={{0,2},{2,4},{4,6},{6,8},{8,10},{10,12},{12,14},{14,0},{1,3},{3,5},... | collective-permute-start | bytes 786440 | tf_op jit(solution)/shard_map/ppermute | solution.py:17
  249.9 8.3 %collective-permute-start.1 = (f32[128,512]{1,0:T(8,128)S(1)}, f32[128,512]{1,0:T(8,128)S(1)}, u32[]{:S(2)}, u32[]{:S(2)}) collective-permute-start(f32[128,512]{1,0:T(8,128)S(1)} %collective-permute-done), channel_id=1, source_target_pairs={{0,2},{2,4},{4,6},{6,8},{8,10},{10,12},{12,14},{14,0},{1,3},{3,5},... | collective-permute-start | bytes 786440 | tf_op jit(solution)/shard_map/ppermute | solution.py:17
  249.9 8.3 %collective-permute-start.4 = (f32[128,512]{1,0:T(8,128)S(1)}, f32[128,512]{1,0:T(8,128)S(1)}, u32[]{:S(2)}, u32[]{:S(2)}) collective-permute-start(f32[128,512]{1,0:T(8,128)S(1)} %multiply_subtract_fusion.1), channel_id=1, source_target_pairs={{0,14},{2,0},{4,2},{6,4},{8,6},{10,8},{12,10},{14,12},{1,15},{3,1}... | collective-permute-start | bytes 786440 | tf_op jit(solution)/shard_map/ppermute | solution.py:19
  258.2 89.3 %collective-permute-start.5 = (f32[128,512]{1,0:T(8,128)S(1)}, f32[128,512]{1,0:T(8,128)S(1)}, u32[]{:S(2)}, u32[]{:S(2)}) collective-permute-start(f32[128,512]{1,0:T(8,128)S(1)} %collective-permute-done.4), channel_id=1, source_target_pairs={{0,14},{2,0},{4,2},{6,4},{8,6},{10,8},{12,10},{14,12},{1,15},{3,1}... | collective-permute-start | bytes 786440 | tf_op jit(solution)/shard_map/ppermute | solution.py:19
  265.8 82.1 %collective-permute-start.3 = (f32[128,512]{1,0:T(8,128)S(1)}, f32[128,512]{1,0:T(8,128)S(1)}, u32[]{:S(2)}, u32[]{:S(2)}) collective-permute-start(f32[128,512]{1,0:T(8,128)S(1)} %collective-permute-done.2), channel_id=1, source_target_pairs={{0,2},{2,4},{4,6},{6,8},{8,10},{10,12},{12,14},{14,0},{1,3},{3,5},... | collective-permute-start | bytes 786440 | tf_op jit(solution)/shard_map/ppermute | solution.py:17
  347.6 8.3 %collective-permute-start.6 = (f32[128,512]{1,0:T(8,128)S(1)}, f32[128,512]{1,0:T(8,128)S(1)}, u32[]{:S(2)}, u32[]{:S(2)}) collective-permute-start(f32[128,512]{1,0:T(8,128)S(1)} %collective-permute-done.5), channel_id=1, source_target_pairs={{0,14},{2,0},{4,2},{6,4},{8,6},{10,8},{12,10},{14,12},{1,15},{3,1}... | collective-permute-start | bytes 786440 | tf_op jit(solution)/shard_map/ppermute | solution.py:19
  369.0 8.5 %collective-permute-start.7 = (f32[128,512]{1,0:T(8,128)S(1)}, f32[128,512]{1,0:T(8,128)S(1)}, u32[]{:S(2)}, u32[]{:S(2)}) collective-permute-start(f32[128,512]{1,0:T(8,128)S(1)} %get-tuple-element.15), channel_id=1, source_target_pairs={{0,2},{2,4},{4,6},{6,8},{8,10},{10,12},{12,14},{14,0},{1,3},{3,5},... | collective-permute-start | bytes 786440 | tf_op jit(solution)/shard_map/ppermute | solution.py:17
  385.0 8.0 %collective-permute-start.9 = (f32[128,512]{1,0:T(8,128)S(1)}, f32[128,512]{1,0:T(8,128)S(1)}, u32[]{:S(2)}, u32[]{:S(2)}) collective-permute-start(f32[128,512]{1,0:T(8,128)S(1)} %collective-permute-done.8), channel_id=1, source_target_pairs={{0,2},{2,4},{4,6},{6,8},{8,10},{10,12},{12,14},{14,0},{1,3},{3,5},... | collective-permute-start | bytes 786440 | tf_op jit(solution)/shard_map/ppermute | solution.py:17
  385.0 8.0 %collective-permute-start.12 = (f32[128,512]{1,0:T(8,128)S(1)}, f32[128,512]{1,0:T(8,128)S(1)}, u32[]{:S(2)}, u32[]{:S(2)}) collective-permute-start(f32[128,512]{1,0:T(8,128)S(1)} %collective-permute-done.11), channel_id=1, source_target_pairs={{0,14},{2,0},{4,2},{6,4},{8,6},{10,8},{12,10},{14,12},{1,15},{3,1}... | collective-permute-start | bytes 786440 | tf_op jit(solution)/shard_map/ppermute | solution.py:19
  393.0 7.8 collective-permute-start.13
  487.0 9.3 %collective-permute-start.14 = (f32[128,512]{1,0:T(8,128)S(1)}, f32[128,512]{1,0:T(8,128)S(1)}, u32[]{:S(2)}, u32[]{:S(2)}) collective-permute-start(f32[128,512]{1,0:T(8,128)S(1)} %broadcast_multiply_fusion), channel_id=1, source_target_pairs={{0,2},{2,4},{4,6},{6,8},{8,10},{10,12},{12,14},{14,0},{1,3},{3,5},... | collective-permute-start | bytes 786440 | tf_op jit(solution)/shard_map/ppermute | solution.py:17
  496.3 8.4 %collective-permute-start.15 = (f32[128,512]{1,0:T(8,128)S(1)}, f32[128,512]{1,0:T(8,128)S(1)}, u32[]{:S(2)}, u32[]{:S(2)}) collective-permute-start(f32[128,512]{1,0:T(8,128)S(1)} %collective-permute-done.14), channel_id=1, source_target_pairs={{0,2},{2,4},{4,6},{6,8},{8,10},{10,12},{12,14},{14,0},{1,3},{3,5},... | collective-permute-start | bytes 786440 | tf_op jit(solution)/shard_map/ppermute | solution.py:17
  496.3 8.4 %collective-permute-start.18 = (f32[128,512]{1,0:T(8,128)S(1)}, f32[128,512]{1,0:T(8,128)S(1)}, u32[]{:S(2)}, u32[]{:S(2)}) collective-permute-start(f32[128,512]{1,0:T(8,128)S(1)} %broadcast_multiply_fusion), channel_id=1, source_target_pairs={{0,14},{2,0},{4,2},{6,4},{8,6},{10,8},{12,10},{14,12},{1,15},{3,1}... | collective-permute-start | bytes 786440 | tf_op jit(solution)/shard_map/ppermute | solution.py:19
  504.7 9.0 %collective-permute-start.19 = (f32[128,512]{1,0:T(8,128)S(1)}, f32[128,512]{1,0:T(8,128)S(1)}, u32[]{:S(2)}, u32[]{:S(2)}) collective-permute-start(f32[128,512]{1,0:T(8,128)S(1)} %collective-permute-done.18), channel_id=1, source_target_pairs={{0,14},{2,0},{4,2},{6,4},{8,6},{10,8},{12,10},{14,12},{1,15},{3,1}... | collective-permute-start | bytes 786440 | tf_op jit(solution)/shard_map/ppermute | solution.py:19
  512.3 7.7 collective-permute-start.17
  513.7 256.8 %reduce-scatter.5.cloned.1.call-start = ((), (), s32[]{:S(2)}) async-start(), calls=%async_computation.6 | async-start | bytes 1179648 | tf_op jit(solution)/shard_map/reduce_scatter | solution.py:77
  609.4 9.2 %collective-permute-start.21 = (f32[128,512]{1,0:T(8,128)S(1)}, f32[128,512]{1,0:T(8,128)S(1)}, u32[]{:S(2)}, u32[]{:S(2)}) collective-permute-start(f32[128,512]{1,0:T(8,128)S(1)} %get-tuple-element.14), channel_id=1, source_target_pairs={{0,2},{2,4},{4,6},{6,8},{8,10},{10,12},{12,14},{14,0},{1,3},{3,5},... | collective-permute-start | bytes 786440 | tf_op jit(solution)/shard_map/ppermute | solution.py:17
  618.7 8.4 %collective-permute-start.22 = (f32[128,512]{1,0:T(8,128)S(1)}, f32[128,512]{1,0:T(8,128)S(1)}, u32[]{:S(2)}, u32[]{:S(2)}) collective-permute-start(f32[128,512]{1,0:T(8,128)S(1)} %collective-permute-done.21), channel_id=1, source_target_pairs={{0,2},{2,4},{4,6},{6,8},{8,10},{10,12},{12,14},{14,0},{1,3},{3,5},... | collective-permute-start | bytes 786440 | tf_op jit(solution)/shard_map/ppermute | solution.py:17
  618.7 8.4 %collective-permute-start.25 = (f32[128,512]{1,0:T(8,128)S(1)}, f32[128,512]{1,0:T(8,128)S(1)}, u32[]{:S(2)}, u32[]{:S(2)}) collective-permute-start(f32[128,512]{1,0:T(8,128)S(1)} %get-tuple-element.14), channel_id=1, source_target_pairs={{0,14},{2,0},{4,2},{6,4},{8,6},{10,8},{12,10},{14,12},{1,15},{3,1}... | collective-permute-start | bytes 786440 | tf_op jit(solution)/shard_map/ppermute | solution.py:19
  634.6 7.8 collective-permute-start.27
  (15 other events, 675.2 us)
Sparse Core Ops, SparseCore 0:
  9.8 77.4 all-gather.3
  97.2 143.1 reduce-scatter.2
  242.1 101.1 all-gather.5
  513.8 83.1 all-gather.7
  735.2 35.1 reduce-scatter.4
